TPU v7x, 256 devices: a whole 4x4x8 slice. The times are simulated.
256 devices in a mesh: station: 64 (over y, x_lo, z), tblock: 4 (over x_hi, core).
Axes of the slice: x: 4 (x_hi: 2, x_lo: 2; x = x_hi * 2 + x_lo), y: 4, z: 8, core: 2. Of those that a mesh axis runs over, the one named last changes fastest.
Arguments:
- voltages: bfloat16 [2, 1024, 262144], P(None, 'station', 'tblock'), may hold values from -127 to 127, as said below
- prototype: float32 [4, 4096], replicated, may hold values from -1.5 to 1.5
Outputs:
- visibilities: bfloat16 [256, 2, 1024, 1024], P(('station', 'tblock'))
Inputs may be any that keep to these rules, and one draw needn't show every extreme that they name: `voltages`: integer-valued samples.
All inputs are finite; a program needn't handle non-finite values.
Results may differ from a plain program's by a relative error of at most 0.0088.
Values may be sent and summed in bfloat16 or wider, within the bound.
A program may use at most 192 MiB of HBM per device.

v0:
```python
import math

import jax
import jax.numpy as jnp
from jax import lax
from jax.sharding import PartitionSpec as P

ROOT = 64
CH_DEV = 1


def passed_along(value, axis, steps):
    count = lax.axis_size(axis)
    first, last = (max(0, -steps), min(count, count - steps))
    return lax.ppermute(value, axis, [(source, source + steps) for source in range(first, last)])


def angles(first_index, second_index, period):
    product = first_index[:, None] * second_index[None, :] % period
    return product.astype(jnp.float32) * (2.0 * math.pi / period)


def transform(subscripts, left_side, table):
    return jnp.einsum(subscripts, left_side, table, preferred_element_type=jnp.float32)


def channel_band(filtered, band_width):
    inputs_here = filtered.shape[1]
    frames = filtered.shape[2]
    points = filtered.shape[3]
    root_size = ROOT
    folded = filtered.reshape(2, inputs_here, frames, root_size, root_size)
    digits = jnp.arange(root_size, dtype=jnp.int32)
    first_angle = angles(digits, digits, root_size)
    cos_first = jnp.cos(first_angle).astype(jnp.bfloat16)
    sin_first = jnp.sin(first_angle).astype(jnp.bfloat16)
    real_section = transform("psab,ac->psbc", folded[0], cos_first) + transform(
        "psab,ac->psbc", folded[1], sin_first
    )
    imag_section = transform("psab,ac->psbc", folded[1], cos_first) - transform(
        "psab,ac->psbc", folded[0], sin_first
    )
    twist_angle = angles(digits, digits, points)
    cos_twist = jnp.cos(twist_angle)
    sin_twist = jnp.sin(twist_angle)
    real_turned = (real_section * cos_twist + imag_section * sin_twist).astype(jnp.bfloat16)
    imag_turned = (imag_section * cos_twist - real_section * sin_twist).astype(jnp.bfloat16)
    lower_edge = (points - band_width) // 2
    first_digit = lower_edge // root_size
    last_digit = (lower_edge + band_width - 1) // root_size
    digit_count = last_digit - first_digit + 1
    high_digits = first_digit + jnp.arange(digit_count, dtype=jnp.int32)
    second_angle = angles(digits, high_digits, root_size)
    cos_second = jnp.cos(second_angle).astype(jnp.bfloat16)
    sin_second = jnp.sin(second_angle).astype(jnp.bfloat16)
    real_out = transform("psbc,bd->sdcp", real_turned, cos_second) + transform(
        "psbc,bd->sdcp", imag_turned, sin_second
    )
    imag_out = transform("psbc,bd->sdcp", imag_turned, cos_second) - transform(
        "psbc,bd->sdcp", real_turned, sin_second
    )
    spectra_all = jnp.stack([real_out, imag_out]).reshape(
        2, frames, digit_count * root_size, inputs_here
    )
    offset_start = lower_edge - first_digit * root_size
    return spectra_all


def correlate(real_rows, imag_rows):
    stacked = jnp.concatenate([real_rows, imag_rows], axis=0)
    turned = jnp.concatenate([imag_rows, -real_rows], axis=0)
    inputs_all = stacked.shape[1]
    contract = (((0,), (0,)), ((), ()))
    products = lax.dot_general(
        jnp.concatenate([stacked, turned], axis=1),
        stacked,
        contract,
        preferred_element_type=jnp.float32,
    )
    return products.reshape(2, inputs_all, inputs_all)


def local(voltages, prototype):
    inputs_here = voltages.shape[1]
    taps_count = prototype.shape[0]
    points = prototype.shape[1]
    root_size = ROOT
    spec_here = voltages.shape[2] // points
    blocks_count = lax.axis_size("tblock")
    band_width = CH_DEV * lax.axis_size("station") * blocks_count
    framed = voltages.reshape(2, inputs_here, spec_here, points)
    earlier = passed_along(framed[:, :, spec_here - (taps_count - 1) :, :], "tblock", 1)
    extended = jnp.concatenate([earlier, framed], axis=2).astype(jnp.float32)
    filtered = prototype[0] * extended[:, :, 0:spec_here, :]
    for tap_index in range(1, taps_count):
        filtered = (
            filtered + prototype[tap_index] * extended[:, :, tap_index : tap_index + spec_here, :]
        )
    band_values = channel_band(filtered.astype(jnp.bfloat16), band_width)
    spectra = (band_values * (1.0 / (32.0 * root_size))).astype(jnp.bfloat16)
    moved = lax.all_to_all(
        lax.all_to_all(spectra, "station", split_axis=2, concat_axis=3, tiled=True),
        "tblock",
        split_axis=2,
        concat_axis=1,
        tiled=True,
    )
    spectra_total = moved.shape[1]
    powers = [correlate(moved[0, :, 0, :], moved[1, :, 0, :])]
    return (jnp.stack(powers) / spectra_total).astype(jnp.bfloat16)


def solution(mesh):
    return jax.shard_map(
        local,
        mesh=mesh,
        in_specs=(P(None, "station", "tblock"), P()),
        out_specs=P(("station", "tblock"), None, None, None),
        check_vma=False,
    )
```

profile of v0, /device:TPU:1, one launch (start us, length us, event | category | flops | bytes accessed | tf_op | source)
XLA Modules:
  0.0 161.4 jit_solution(1144172215406844177)
XLA Ops:
  0.0 4.5 %copy.62 = bf16[4,8,16,4096]{3,2,1,0:T(8,128)(2,1)S(1)} copy(bf16[4,8,16,4096]{3,1,2,0:T(8,128)(2,1)} %bitcast.76) | data formatting | bytes 8388608
  5.7 6.2 %collective-permute-start = (bf16[2,16,3,4096]{3,1,2,0:T(8,128)(2,1)S(1)}, bf16[2,16,3,4096]{3,1,2,0:T(8,128)(2,1)S(1)}, u32[]{:S(2)}, u32[]{:S(2)}) collective-permute-start(bf16[2,16,3,4096]{3,1,2,0:T(8,128)(2,1)S(1)} %copy.38), channel_id=1, source_target_pairs={{0,1},{1,2},{2,3},{4,5},{5,6},{6,7},{8,9},{9,10},{10,11},{12,13},{... | collective-permute-start | bytes 2359304 | tf_op jit(solution)/shard_map/ppermute | solution.py:15
  12.2 8.5 %collective-permute-done = bf16[2,16,3,4096]{3,1,2,0:T(8,128)(2,1)S(1)} collective-permute-done((bf16[2,16,3,4096]{3,1,2,0:T(8,128)(2,1)S(1)}, bf16[2,16,3,4096]{3,1,2,0:T(8,128)(2,1)S(1)}, u32[]{:S(2)}, u32[]{:S(2)}) %collective-permute-start) | collective-permute-done | bytes 786464 | tf_op jit(solution)/shard_map/ppermute | solution.py:15
  21.4 6.6 %maximum_convert_fusion = f32[2,16,19,4096]{3,2,1,0:T(8,128)} fusion(bf16[2,16,16,4096]{3,2,1,0:T(8,128)(2,1)S(1)} %bitcast.73, bf16[2,16,3,4096]{3,2,1,0:T(4,128)(2,1)S(1)} %copy.39), kind=kLoop, calls=%fused_computation.11 | loop fusion | flops 9961472 | bytes 14942208 | tf_op jit(solution)/shard_map/convert_element_type | solution.py:93
  28.0 20.1 %fusion.1 = bf16[2,16,16,4096]{3,2,1,0:T(8,128)(2,1)} fusion(f32[2,16,19,4096]{3,2,1,0:T(8,128)} %maximum_convert_fusion, f32[4096]{0:T(1024)S(1)} %bitcast.82, f32[4096]{0:T(1024)S(1)} %bitcast.83, f32[4096]{0:T(1024)S(1)} %bitcast.81, f32[4096]{0:T(1024)S(1)} %bitcast.80), kind=kLoop, calls=%fused_computation.2 | loop fusion | flops 16777216 | bytes 37814272 | tf_op jit(solution)/shard_map/convert_element_type | solution.py:99
  48.1 3.9 %fusion.84 = (bf16[1,16,16,4096]{3,2,1,0:T(8,128)(2,1)}, bf16[1,16,16,4096]{3,2,1,0:T(8,128)(2,1)S(1)}) fusion(bf16[2,16,16,4096]{3,2,1,0:T(8,128)(2,1)} %fusion.1), kind=kLoop, calls=%fused_computation.103 | loop fusion | bytes 8388608 | tf_op jit(solution)/shard_map/slice | solution.py:37
  52.1 6.9 %squeeze.14 = bf16[16,16,64,64]{3,2,1,0:T(8,128)(2,1)} reshape(bf16[1,16,16,4096]{3,2,1,0:T(8,128)(2,1)} %get-tuple-element.7) | data formatting | bytes 4194304 | tf_op jit(solution)/shard_map/squeeze | solution.py:37
  58.9 7.0 %fusion.32 = f32[16,16,64,64]{3,2,1,0:T(8,128)} fusion(bf16[16,16,64,64]{3,2,1,0:T(8,128)(2,1)} %squeeze.14), kind=kOutput, calls=%fused_computation.52 | convolution fusion | flops 134279168 | bytes 6291456 | tf_op jit(solution)/shard_map/psab,ac->psbc/dot_general | solution.py:24
  65.9 4.6 %fusion.38 = f32[16,16,64,64]{3,2,1,0:T(8,128)} fusion(bf16[16,16,64,64]{3,2,1,0:T(8,128)(2,1)S(1)} %copy-done), kind=kOutput, calls=%fused_computation.55 | convolution fusion | flops 134279168 | bytes 6291456 | tf_op jit(solution)/shard_map/psab,ac->psbc/dot_general | solution.py:24
  70.5 5.5 %squeeze.15 = bf16[16,16,64,64]{3,2,1,0:T(8,128)(2,1)} reshape(bf16[1,16,16,4096]{3,2,1,0:T(8,128)(2,1)S(1)} %get-tuple-element.8) | data formatting | bytes 4194304 | tf_op jit(solution)/shard_map/squeeze | solution.py:38
  76.0 7.0 %fusion.34 = f32[16,16,64,64]{3,2,1,0:T(8,128)} fusion(bf16[16,16,64,64]{3,2,1,0:T(8,128)(2,1)} %squeeze.15), kind=kOutput, calls=%fused_computation.53 | convolution fusion | flops 134279168 | bytes 6291456 | tf_op jit(solution)/shard_map/psab,ac->psbc/dot_general | solution.py:24
  83.0 13.5 %add_convert_fusion = (bf16[16,16,64,64]{3,2,1,0:T(8,128)(2,1)}, bf16[16,16,64,64]{3,2,1,0:T(8,128)(2,1)}) fusion(f32[64,64]{1,0:T(8,128)S(1)} %get-tuple-element.15, f32[64,64]{1,0:T(8,128)S(1)} %get-tuple-element.16, f32[16,16,64,64]{3,2,1,0:T(8,128)} %fusion.32, f32[16,16,64,64]{3,2,1,0:T(8,128)S(1)} %copy-done.1, f32[16,16,64,64]{3,2,1,0:T(8,128)} %fusion.34, ...), kind=kOutput, calls=%fused_computation.10 | convolution fusion | flops 144764928 | bytes 18907136 | tf_op jit(solution)/shard_map/psab,ac->psbc/dot_general | solution.py:24
  96.5 3.1 %fusion.49 = f32[4,16,16,64]{3,0,2,1:T(4,128)S(1)} fusion(bf16[16,16,64,64]{3,2,1,0:T(8,128)(2,1)} %get-tuple-element.5, s32[4]{0:T(128)S(1)} %iota_add_fusion), kind=kOutput, calls=%fused_computation.67 | convolution fusion | flops 8392448 | bytes 2359312 | tf_op jit(solution)/shard_map/psbc,bd->sdcp/dot_general | solution.py:24
  99.6 3.0 %fusion.47 = f32[4,16,16,64]{3,0,2,1:T(4,128)S(1)} fusion(bf16[16,16,64,64]{3,2,1,0:T(8,128)(2,1)} %get-tuple-element.6, s32[4]{0:T(128)S(1)} %iota_add_fusion), kind=kOutput, calls=%fused_computation.66 | convolution fusion | flops 8392448 | bytes 2359312 | tf_op jit(solution)/shard_map/psbc,bd->sdcp/dot_general | solution.py:24
  102.6 0.8 fusion.5
  103.9 2.9 %fusion.4 = f32[16,4,64,16]{2,1,0,3:T(4,128)S(1)} fusion(f32[4,16,16,64]{3,0,2,1:T(4,128)S(1)} %fusion.47, bf16[16,16,64,64]{3,2,1,0:T(8,128)(2,1)} %get-tuple-element.5, s32[4]{0:T(128)S(1)} %iota_add_fusion), kind=kOutput, calls=%fused_computation.13 | convolution fusion | flops 8457984 | bytes 2621456 | tf_op jit(solution)/shard_map/psbc,bd->sdcp/dot_general | solution.py:24
  107.4 3.0 %copy.46 = bf16[2,16,256,16]{3,1,0,2:T(8,128)(2,1)S(1)} copy(bf16[2,16,256,16]{2,3,1,0:T(8,128)(2,1)S(1)} %fusion.6) | data formatting | bytes 524288 | tf_op jit(solution)/shard_map/convert_element_type | solution.py:100
  110.3 2.3 %reshape.86 = bf16[64,2,1024]{2,1,0:T(2,128)(2,1)S(1)} reshape(bf16[256,2,16,16]{3,2,1,0:T(8,128)(2,1)S(1)} %bitcast.74) | data formatting | bytes 524288
  112.6 22.7 %all_to_all.33 = bf16[64,2,1024]{2,1,0:T(2,128)(2,1)S(1)} all-to-all(bf16[64,2,1024]{2,1,0:T(2,128)(2,1)S(1)} %reshape.86), channel_id=1, replica_groups=mesh['station'=64,'tblock'=4] {'station'}, dimensions={0} | all-to-all | bytes 524288 | tf_op jit(solution)/shard_map/all_to_all | solution.py:102
  135.3 1.4 reshape.87
  136.7 2.7 %copy.60 = bf16[2,16,4,64,16]{4,3,1,0,2:T(8,128)(2,1)} copy(bf16[2,16,4,64,16]{4,1,0,2,3:T(8,128)(2,1)S(1)} %bitcast.75) | data formatting | bytes 524288 | tf_op jit(solution)/shard_map/all_to_all | solution.py:102
  139.4 4.7 %reshape.85 = bf16[2,16,4,1024]{3,1,0,2:T(8,128)(2,1)S(1)} reshape(bf16[2,16,4,64,16]{4,3,1,0,2:T(8,128)(2,1)} %copy.60) | data formatting | bytes 524288 | tf_op jit(solution)/shard_map/all_to_all | solution.py:102
  144.1 14.0 %all_to_all.34 = bf16[2,16,4,1024]{3,1,0,2:T(8,128)(2,1)S(1)} all-to-all(bf16[2,16,4,1024]{3,1,0,2:T(8,128)(2,1)S(1)} %reshape.85), channel_id=1, replica_groups=mesh['station'=64,'tblock'=4] {'tblock'}, dimensions={2} | all-to-all | bytes 524288 | tf_op jit(solution)/shard_map/all_to_all | solution.py:101
  158.1 3.3 %multiply_convert_fusion = bf16[2048,1024]{1,0:T(8,128)(2,1)} fusion(bf16[64,1024]{1,0:T(8,128)(2,1)S(1)} %bitcast_negate_fusion, bf16[64,1024]{1,0:T(8,128)(2,1)S(1)} %bitcast.79, bf16[64,1024]{1,0:T(8,128)(2,1)S(1)} %bitcast.78), kind=kOutput, calls=%fused_computation.8 | convolution fusion | flops 543686656 | bytes 4587520 | tf_op jit(solution)/shard_map/dot_general | solution.py:74
  (22 shorter events, 3.2 us)
Async XLA Ops:
  0.0 12.1 %copy-start.3 = (f32[4,4096]{1,0:T(4,128)S(1)}, f32[4,4096]{1,0:T(4,128)}, u32[]{:S(2)}) copy-start(f32[4,4096]{1,0:T(4,128)} %param.3) | copy-start | bytes 196612
  5.7 15.0 %collective-permute-start = (bf16[2,16,3,4096]{3,1,2,0:T(8,128)(2,1)S(1)}, bf16[2,16,3,4096]{3,1,2,0:T(8,128)(2,1)S(1)}, u32[]{:S(2)}, u32[]{:S(2)}) collective-permute-start(bf16[2,16,3,4096]{3,1,2,0:T(8,128)(2,1)S(1)} %copy.38), channel_id=1, source_target_pairs={{0,1},{1,2},{2,3},{4,5},{5,6},{6,7},{8,9},{9,10},{10,11},{12,13},{... | collective-permute-start | bytes 2359304 | tf_op jit(solution)/shard_map/ppermute | solution.py:15
  58.9 7.0 %copy-start = (bf16[16,16,64,64]{3,2,1,0:T(8,128)(2,1)S(1)}, bf16[16,16,64,64]{3,2,1,0:T(8,128)(2,1)}, u32[]{:S(2)}) copy-start(bf16[16,16,64,64]{3,2,1,0:T(8,128)(2,1)} %squeeze.14) | copy-start | bytes 6291460
  76.0 7.0 %copy-start.1 = (f32[16,16,64,64]{3,2,1,0:T(8,128)S(1)}, f32[16,16,64,64]{3,2,1,0:T(8,128)}, u32[]{:S(2)}) copy-start(f32[16,16,64,64]{3,2,1,0:T(8,128)} %fusion.38) | copy-start | bytes 12582916
  96.5 6.0 %copy-start.2 = (bf16[16,16,64,64]{3,2,1,0:T(8,128)(2,1)S(1)}, bf16[16,16,64,64]{3,2,1,0:T(8,128)(2,1)}, u32[]{:S(2)}) copy-start(bf16[16,16,64,64]{3,2,1,0:T(8,128)(2,1)} %get-tuple-element.6) | copy-start | bytes 6291460
where the time goes:
time: 162 us; the launch traced here: 161 us
  matrix products  45.1 us (28%)
  local copies, waits for them, and re-layouts  37.8 us (23%)
  blocking collectives  36.6 us (23%)
  other arithmetic  27 us (17%)
  waiting for transfers between devices  8.51 us (5%)
  starting transfers between devices  6.22 us (4%)
    dot_general x8, matrix products, transform(): jnp.einsum(subscripts, left_side, table, preferred_element_type=jnp.float32)  41.8 us
    all_to_all x1, blocking collectives, local(): lax.all_to_all(spectra, 'station', split_axis=2, concat_axis=3, tiled=True)  22.7 us
    convert_element_type x1, other arithmetic, local(): band_values = channel_band(filtered.astype(jnp.bfloat16), band_width)  20.1 us
    all_to_all x1, blocking collectives, local(): lax.all_to_all(lax.all_to_all(spectra, 'station', split_axis=2, concat_ax...  14 us
    ppermute x1, waiting for transfers between devices, passed_along(): lax.ppermute(value, axis, [(source, source + steps) for source in range(f...  8.51 us
    unnamed x11, local copies, waits for them, and re-layouts  8.24 us
    all_to_all x2, local copies, waits for them, and re-layouts, local(): lax.all_to_all(spectra, 'station', split_axis=2, concat_axis=3, tiled=True)  7.37 us
    squeeze x1, local copies, waits for them, and re-layouts, channel_band(): folded[0]  6.88 us
  transfers between devices with their start and end apart: 1, of which 1 were waited for; matrix products, arithmetic and copies ran while one was open for 0% of the time, Pallas kernels for 0%

commit v1 on v0

v1 whole, which is shorter than its diff:
```python
import math

import jax
import jax.numpy as jnp
import ml_dtypes
import numpy as np
from jax import lax
from jax.experimental import pallas as pl
from jax.experimental.pallas import tpu as pltpu
from jax.sharding import PartitionSpec as P

ROOT = 64
NFFT = 4096
TAPS = 4
BAND = 256
FRAMES = 16
INPUTS = 16
ROWS = FRAMES * INPUTS
EDGE = TAPS - 1
EDGE_ROWS = 64
STATIONS = 64
BLOCKS = 4
DEVICES = STATIONS * BLOCKS
LANES = 128
STEP = 128
MESH = pl.DeviceIdType.MESH


def channel_table():
    def angles(first, second, period):
        product = (first[:, None] * second[None, :]) % period
        return product.astype(np.float32) * np.float32(2.0 * math.pi / period)

    def rounded(values):
        return values.astype(ml_dtypes.bfloat16).astype(np.float64)

    digits = np.arange(ROOT)
    first = angles(digits, digits, ROOT)
    root = rounded(np.cos(first)) - 1j * rounded(np.sin(first))
    twist_angle = angles(digits, digits, NFFT)
    twist = np.cos(twist_angle).astype(np.float64) - 1j * np.sin(twist_angle).astype(np.float64)
    high = (NFFT - BAND) // 2 // ROOT + np.arange(BAND // ROOT)
    table = (
        root.T[None, :, :, None] * twist.T[None, :, None, :] * root[:, high].T[:, None, None, :]
    )
    table = table.reshape(BAND, NFFT) / (32.0 * ROOT)
    return np.concatenate([table.real, table.imag]).astype(np.float32).astype(ml_dtypes.bfloat16)


def device(index):
    return (lax.div(index, BLOCKS), lax.rem(index, BLOCKS))


def exchange_kernel(
    v_hbm,
    proto_ref,
    w_hbm,
    out_ref,
    v_buf,
    w_buf,
    x_buf,
    xe_buf,
    rows_buf,
    edge_out,
    edge_in,
    send_buf,
    v_sem,
    w_sem,
    edge_send,
    edge_recv,
    send_sem,
    recv_sem,
):
    station = lax.axis_index("station")
    block = lax.axis_index("tblock")
    me = station * BLOCKS + block

    frame_order = list(range(FRAMES - EDGE, FRAMES)) + list(range(FRAMES - EDGE))
    frame_copies = {}
    for f in frame_order:
        here = pl.ds(f * NFFT, NFFT)
        frame_copies[f] = pltpu.make_async_copy(
            v_hbm.at[:, :, here], v_buf.at[:, :, here], v_sem.at[f]
        )
        frame_copies[f].start()
    w_copy = pltpu.make_async_copy(w_hbm, w_buf, w_sem)
    w_copy.start()

    barrier = pltpu.get_barrier_semaphore()

    def greet(k, carry):
        other = lax.rem(me + k, DEVICES)
        pl.semaphore_signal(barrier, inc=1, device_id=device(other), device_id_type=MESH)
        return carry

    lax.fori_loop(1, DEVICES, greet, 0, unroll=5)

    for f in frame_order:
        frame_copies[f].wait()

    def filter_step(k, carry):
        lanes = pl.ds(pl.multiple_of(k * STEP, STEP), STEP)
        taps = [proto_ref[pl.ds(t, 1), lanes] for t in range(TAPS)]
        for part in range(2):
            window = {}
            for s in range(FRAMES + EDGE):
                if s < FRAMES:
                    at = pl.ds(pl.multiple_of(s * NFFT + k * STEP, STEP), STEP)
                    window[s] = v_buf[part, :, at].astype(jnp.float32)
                total = None
                for t in range(TAPS):
                    f = s + t - EDGE
                    if 0 <= f < FRAMES:
                        term = taps[t] * window[f]
                        total = term if total is None else total + term
                value = total.astype(jnp.bfloat16)
                if s < FRAMES:
                    x_buf[pl.ds(part * ROWS + s * INPUTS, INPUTS), lanes] = value
                else:
                    row = part * EDGE_ROWS + (s - FRAMES) * INPUTS
                    xe_buf[pl.ds(row, INPUTS), lanes] = value
            pad = part * EDGE_ROWS + EDGE * INPUTS
            xe_buf[pl.ds(pad, INPUTS), lanes] = jnp.zeros((INPUTS, STEP), jnp.bfloat16)
        return carry

    lax.fori_loop(0, NFFT // STEP, filter_step, 0)

    w_copy.wait()
    contract = (((1,), (1,)), ((), ()))
    edge = lax.dot_general(w_buf[...], xe_buf[...], contract, preferred_element_type=jnp.float32)
    lane = lax.broadcasted_iota(jnp.int32, (BAND, LANES), 1)
    turned = pltpu.roll(edge[BAND:], EDGE_ROWS, 1)
    edge = edge[:BAND] + jnp.where(lane < EDGE_ROWS, -turned, turned)
    edge_out[...] = edge.astype(jnp.bfloat16)

    pl.semaphore_wait(barrier, DEVICES - 1)

    after = (station, lax.min(block + 1, BLOCKS - 1))
    edge_copy = pltpu.make_async_remote_copy(
        src_ref=edge_out,
        dst_ref=edge_in,
        send_sem=edge_send,
        recv_sem=edge_recv,
        device_id=after,
        device_id_type=MESH,
    )

    @pl.when(block < BLOCKS - 1)
    def _():
        edge_copy.start()

    @pl.when(block == 0)
    def _():
        edge_in[...] = jnp.zeros_like(edge_in)

    main = lax.dot_general(w_buf[...], x_buf[...], contract, preferred_element_type=jnp.float32)
    real = main[:BAND, :ROWS] - main[BAND:, ROWS:]
    imag = main[BAND:, :ROWS] + main[:BAND, ROWS:]

    @pl.when(block > 0)
    def _():
        edge_copy.wait_recv()

    carried = edge_in[...].astype(jnp.float32)
    real_edge = jnp.where(lane < EDGE_ROWS, carried, 0.0)
    imag_edge = jnp.where(lane < EDGE_ROWS, pltpu.roll(carried, EDGE_ROWS, 1), 0.0)
    pieces = [
        real[:, :LANES] + real_edge,
        real[:, LANES:],
        imag[:, :LANES] + imag_edge,
        imag[:, LANES:],
    ]
    for r in range(4):
        rows_buf[pl.ds(r, BAND, stride=4), :] = pieces[r]
    send_buf[...] = rows_buf[...].reshape(BAND, 4, LANES).astype(jnp.bfloat16)

    own = pltpu.make_async_copy(send_buf.at[me], out_ref.at[me], recv_sem)
    own.start()

    def go(k, carry):
        other = lax.rem(me + k, DEVICES)
        pltpu.make_async_remote_copy(
            src_ref=send_buf.at[other],
            dst_ref=out_ref.at[me],
            send_sem=send_sem,
            recv_sem=recv_sem,
            device_id=device(other),
            device_id_type=MESH,
        ).start()
        return carry

    lax.fori_loop(1, DEVICES, go, 0, unroll=5)

    @pl.when(block < BLOCKS - 1)
    def _():
        edge_copy.wait_send()

    sent = send_buf.at[pl.ds(0, DEVICES - 1)]
    pltpu.make_async_copy(sent, sent, send_sem).wait()
    pltpu.make_async_copy(out_ref, out_ref, recv_sem).wait()


def exchange(voltages, prototype, table):
    return pl.pallas_call(
        exchange_kernel,
        out_shape=jax.ShapeDtypeStruct((DEVICES, 4, LANES), jnp.bfloat16),
        in_specs=[
            pl.BlockSpec(memory_space=pl.ANY),
            pl.BlockSpec(memory_space=pltpu.VMEM),
            pl.BlockSpec(memory_space=pl.ANY),
        ],
        out_specs=pl.BlockSpec(memory_space=pl.ANY),
        scratch_shapes=[
            pltpu.VMEM((2, INPUTS, FRAMES * NFFT), jnp.bfloat16),
            pltpu.VMEM((2 * BAND, NFFT), jnp.bfloat16),
            pltpu.VMEM((2 * ROWS, NFFT), jnp.bfloat16),
            pltpu.VMEM((2 * EDGE_ROWS, NFFT), jnp.bfloat16),
            pltpu.VMEM((4 * BAND, LANES), jnp.float32),
            pltpu.VMEM((BAND, LANES), jnp.bfloat16),
            pltpu.VMEM((BAND, LANES), jnp.bfloat16),
            pltpu.VMEM((DEVICES, 4, LANES), jnp.bfloat16),
            pltpu.SemaphoreType.DMA((FRAMES,)),
            pltpu.SemaphoreType.DMA,
            pltpu.SemaphoreType.DMA,
            pltpu.SemaphoreType.DMA,
            pltpu.SemaphoreType.DMA,
            pltpu.SemaphoreType.DMA,
        ],
        compiler_params=pltpu.CompilerParams(
            collective_id=0, has_side_effects=True, vmem_limit_bytes=40 * 1024 * 1024
        ),
        name="channelize_and_send",
    )(voltages, prototype, table)


def correlate_kernel(moved_ref, out_ref, wide, gathered, left, right):
    rows = out_ref.shape[2]
    step = pl.program_id(0)

    @pl.when(step == 0)
    def _():
        wide[...] = moved_ref[...].astype(jnp.float32).reshape(DEVICES * 4, LANES)
        spot = lax.broadcasted_iota(jnp.int32, (8, LANES), 1) // INPUTS
        row = lax.broadcasted_iota(jnp.int32, (8, LANES), 0)
        source = lax.rem(spot - row + 8, 8)
        back = lax.rem(lax.broadcasted_iota(jnp.int32, (8, LANES), 1) + row * INPUTS, LANES)
        for group in range(8):
            for q in range(16):
                tile = wide[pl.ds(group * 128 + q, 8, stride=16), :]
                tile = pltpu.roll(tile, 0, 1, stride=INPUTS, stride_axis=0)
                tile = jnp.take_along_axis(tile, source, axis=0)
                tile = jnp.take_along_axis(tile, back, axis=1)
                tb, part, half = q // 4, q // 2 % 2, q % 2
                at = part * 64 + (tb * 2 + half) * 8
                gathered[pl.ds(at, 8), pl.ds(group * LANES, LANES)] = tile
        right[...] = gathered[...].astype(jnp.bfloat16)
        lane = lax.broadcasted_iota(jnp.int32, (LANES, LANES), 1)
        for group in range(8):
            square = gathered[:, pl.ds(group * LANES, LANES)].T
            other = pltpu.roll(square, 64, 1)
            left[0, pl.ds(group * LANES, LANES), :] = square.astype(jnp.bfloat16)
            left[1, pl.ds(group * LANES, LANES), :] = jnp.where(lane < 64, other, -other).astype(
                jnp.bfloat16
            )

    here = pl.ds(pl.multiple_of(step * rows, rows), rows)
    for part in range(2):
        product = jnp.dot(left[part, here, :], right[...], preferred_element_type=jnp.float32)
        out_ref[0, part] = (product * (1.0 / 64.0)).astype(jnp.bfloat16)


def correlate(moved):
    everyone = STATIONS * INPUTS
    rows = 128
    return pl.pallas_call(
        correlate_kernel,
        grid=(everyone // rows,),
        out_shape=jax.ShapeDtypeStruct((1, 2, everyone, everyone), jnp.bfloat16),
        in_specs=[pl.BlockSpec((DEVICES, 4, LANES), lambda i: (0, 0, 0))],
        out_specs=pl.BlockSpec((1, 2, rows, everyone), lambda i: (0, 0, i, 0)),
        scratch_shapes=[
            pltpu.VMEM((DEVICES * 4, LANES), jnp.float32),
            pltpu.VMEM((LANES, everyone), jnp.float32),
            pltpu.VMEM((2, everyone, LANES), jnp.bfloat16),
            pltpu.VMEM((LANES, everyone), jnp.bfloat16),
        ],
        compiler_params=pltpu.CompilerParams(vmem_limit_bytes=32 * 1024 * 1024),
        name="correlate",
    )(moved)


def local(voltages, prototype):
    table = jnp.asarray(channel_table())
    return correlate(exchange(voltages, prototype, table))


def solution(mesh):
    return jax.shard_map(
        local,
        mesh=mesh,
        in_specs=(P(None, "station", "tblock"), P()),
        out_specs=P(("station", "tblock"), None, None, None),
        check_vma=False,
    )
```

time: 162 us -> 40.3 us (0.25)
  matrix products: 45.1 us -> 0 us
  blocking collectives: 36.6 us -> 0 us
  Pallas kernels: 0 us -> 34.9 us
  local copies, waits for them, and re-layouts: 37.8 us -> 5.21 us
  other arithmetic: 27 us -> 0 us
  waiting for transfers between devices: 8.51 us -> 0 us
  starting transfers between devices: 6.22 us -> 0 us
    dot_general x9 -> x0, matrix products: 45.1 us -> none  [the longest x8 41.8 us: transform(): jnp.einsum(subscripts, left_side, table, preferred_element_type=jnp.float32)]
    all_to_all x2 -> x0, blocking collectives: 36.6 us -> none  [the longest x1 22.7 us: local(): lax.all_to_all(spectra, 'station', split_axis=2, concat_axis=3, tiled=True)]
    pallas_call x0 -> x2, Pallas kernels: none -> 34.9 us  [the longest x1 29.5 us: exchange(): pl.pallas_call(exchange_kernel, out_shape=jax.ShapeDtypeStruct((DEVICES,...]
    convert_element_type x3 -> x0, other arithmetic: 26.8 us -> none  [the longest x1 20.1 us: local(): band_values = channel_band(filtered.astype(jnp.bfloat16), band_width)]
    squeeze x2 -> x0, local copies, waits for them, and re-layouts: 12.4 us -> none  [the longest x1 6.88 us: channel_band(): folded[0]]
    ppermute x1 -> x0, waiting for transfers between devices: 8.51 us -> none  [passed_along(): lax.ppermute(value, axis, [(source, source + steps) for source in range(f...]
    all_to_all x3 -> x0, local copies, waits for them, and re-layouts: 7.38 us -> none  [the longest x2 7.37 us: local(): lax.all_to_all(spectra, 'station', split_axis=2, concat_axis=3, tiled=True)]
    ppermute x1 -> x0, starting transfers between devices: 6.22 us -> none  [passed_along(): lax.ppermute(value, axis, [(source, source + steps) for source in range(f...]
  transfers between devices with their start and end apart: 1 -> 0, of which waited for: 1 -> 0; matrix products, arithmetic and copies ran while one was open for 0% -> 0% of each run, Pallas kernels for 0% -> 0%
where the time goes in v1:
time: 40.3 us; the launch traced here: 40.1 us
  Pallas kernels  34.9 us (87%)
  local copies, waits for them, and re-layouts  5.21 us (13%)
    pallas_call x1, Pallas kernels, exchange(): pl.pallas_call(exchange_kernel, out_shape=jax.ShapeDtypeStruct((DEVICES,...  29.5 us
    pallas_call x1, Pallas kernels, correlate(): pl.pallas_call(correlate_kernel, grid=(everyone // rows,), out_shape=jax....  5.37 us
    unnamed x6, local copies, waits for them, and re-layouts  5.21 us

profile of v1, /device:TPU:1, one launch (start us, length us, event | category | flops | bytes accessed | tf_op | source)
XLA Modules:
  0.0 40.1 jit_solution(8781638081406352394)
XLA Ops:
  0.0 0.0 copy-start
  0.0 2.2 %copy-done = bf16[2,16,65536]{2,1,0:T(8,128)(2,1)S(1)} copy-done((bf16[2,16,65536]{2,1,0:T(8,128)(2,1)S(1)}, bf16[2,16,65536]{2,1,0:T(8,128)(2,1)}, u32[]{:S(2)}) %copy-start) | copy-done | bytes 4194328
  2.2 0.0 copy-start.1
  2.2 2.2 %copy-done.1 = bf16[512,4096]{1,0:T(8,128)(2,1)S(1)} copy-done((bf16[512,4096]{1,0:T(8,128)(2,1)S(1)}, bf16[512,4096]{1,0:T(8,128)(2,1)}, u32[]{:S(2)}) %copy-start.1) | copy-done | bytes 4194328
  4.4 0.0 copy-start.2
  4.4 0.8 %copy-done.2 = f32[4,4096]{1,0:T(4,128)S(1)} copy-done((f32[4,4096]{1,0:T(4,128)S(1)}, f32[4,4096]{1,0:T(4,128)}, u32[]{:S(2)}) %copy-start.2) | copy-done | bytes 65560
  5.2 29.5 %channelize_and_send.1.moved_ref = bf16[256,4,128]{2,1,0:T(4,128)(2,1)S(1)} custom-call(bf16[2,16,65536]{2,1,0:T(8,128)(2,1)S(1)} %copy-done, f32[4,4096]{1,0:T(4,128)S(1)} %copy-done.2, bf16[512,4096]{1,0:T(8,128)(2,1)S(1)} %copy-done.1), custom_call_target="tpu_custom_call" | custom-call | tf_op jit(solution)/shard_map/channelize_and_send/pallas_call | solution.py:204
  34.7 5.4 %correlate.1 = bf16[1,2,1024,1024]{3,2,1,0:T(8,128)(2,1)} custom-call(bf16[256,4,128]{2,1,0:T(4,128)(2,1)S(1)} %channelize_and_send.1.moved_ref), custom_call_target="tpu_custom_call" | custom-call | tf_op jit(solution)/shard_map/correlate/pallas_call | solution.py:275
Async XLA Ops:
  0.0 2.2 %copy-start = (bf16[2,16,65536]{2,1,0:T(8,128)(2,1)S(1)}, bf16[2,16,65536]{2,1,0:T(8,128)(2,1)}, u32[]{:S(2)}) copy-start(bf16[2,16,65536]{2,1,0:T(8,128)(2,1)} %v_hbm.1) | copy-start | bytes 12582916
  2.2 2.2 %copy-start.1 = (bf16[512,4096]{1,0:T(8,128)(2,1)S(1)}, bf16[512,4096]{1,0:T(8,128)(2,1)}, u32[]{:S(2)}) copy-start(bf16[512,4096]{1,0:T(8,128)(2,1)} %constant.2.clone.w_hbm) | copy-start | bytes 12582916
  4.4 0.8 %copy-start.2 = (f32[4,4096]{1,0:T(4,128)S(1)}, f32[4,4096]{1,0:T(4,128)}, u32[]{:S(2)}) copy-start(f32[4,4096]{1,0:T(4,128)} %proto_ref.1) | copy-start | bytes 196612

commit v2 on v1

v2 whole, which is shorter than its diff:
```python
import math

import jax
import jax.numpy as jnp
import ml_dtypes
import numpy as np
from jax import lax
from jax.experimental import pallas as pl
from jax.experimental.pallas import tpu as pltpu
from jax.sharding import PartitionSpec as P

ROOT = 64
NFFT = 4096
TAPS = 4
BAND = 256
FRAMES = 16
INPUTS = 16
EDGE = TAPS - 1
QUAD = 4
QUAD_ROWS = QUAD * INPUTS
STATIONS = 64
BLOCKS = 4
DEVICES = STATIONS * BLOCKS
LANES = 128
CHUNK = 512
CHUNKS = NFFT // CHUNK
HALF = BAND // 2
MESH = pl.DeviceIdType.MESH
CONTRACT = (((1,), (1,)), ((), ()))


def channel_table():
    def angles(first, second, period):
        product = (first[:, None] * second[None, :]) % period
        return product.astype(np.float32) * np.float32(2.0 * math.pi / period)

    def rounded(values):
        return values.astype(ml_dtypes.bfloat16).astype(np.float64)

    digits = np.arange(ROOT)
    first = angles(digits, digits, ROOT)
    root = rounded(np.cos(first)) - 1j * rounded(np.sin(first))
    twist_angle = angles(digits, digits, NFFT)
    twist = np.cos(twist_angle).astype(np.float64) - 1j * np.sin(twist_angle).astype(np.float64)
    high = (NFFT - BAND) // 2 // ROOT + np.arange(BAND // ROOT)
    table = (
        root.T[None, :, :, None] * twist.T[None, :, None, :] * root[:, high].T[:, None, None, :]
    )
    table = table.reshape(BAND, NFFT) / (32.0 * ROOT)
    return np.concatenate([table.real, table.imag]).astype(np.float32).astype(ml_dtypes.bfloat16)


def far_first(step, size):
    return size // 2 + (1 - 2 * (step % 2)) * ((step + 1) // 2)


class Partners:
    def __init__(self):
        station = lax.axis_index("station")
        block = lax.axis_index("tblock")
        self.z = lax.rem(station, 8)
        x = lax.div(block, 2) * 2 + lax.rem(lax.div(station, 8), 2)
        y = lax.div(station, 16)
        core = lax.rem(block, 2)
        xs, ys = {}, {}
        for d in range(4):
            there = lax.rem(x + d, 4)
            xs[d] = (lax.rem(there, 2) * 8, lax.div(there, 2) * 2)
            ys[d] = lax.rem(y + d, 4) * 16
        offsets = [(dx, dy, dc) for dx in range(4) for dy in range(4) for dc in (1, 0)]
        offsets.sort(key=lambda o: -(min(o[0], 4 - o[0]) + min(o[1], 4 - o[1])))
        self.plane = []
        for dx, dy, dc in offsets:
            low, high = xs[dx]
            self.plane.append((ys[dy] + low, high + (core if dc == 0 else 1 - core)))

    def layer(self, step):
        if isinstance(step, int):
            shift = far_first(step, 8)
        else:
            odd = lax.rem(step, 2)
            shift = 4 + (1 - 2 * odd) * lax.div(step + 1, 2)
        z = lax.rem(self.z + shift, 8)
        found = [(base + z, block) for base, block in self.plane]
        return found[:-1] if isinstance(step, int) and step == 7 else found


def exchange_kernel(
    v_hbm,
    proto_hbm,
    w_hbm,
    late_out,
    early_out,
    proto_ref,
    v_buf,
    w_buf,
    x_even,
    x_odd,
    total,
    rows_buf,
    late_send,
    early_send,
    proto_sem,
    chunk_sem,
    late_send_sem,
    late_recv_sem,
    early_send_sem,
    early_recv_sem,
):
    station = lax.axis_index("station")
    block = lax.axis_index("tblock")
    me = station * BLOCKS + block
    slots = (x_even, x_odd)

    proto_copy = pltpu.make_async_copy(proto_hbm, proto_ref, proto_sem)
    proto_copy.start()
    for k in range(CHUNKS):
        lanes = pl.ds(k * CHUNK, CHUNK)
        pltpu.make_async_copy(w_hbm.at[:, lanes], w_buf.at[:, lanes], chunk_sem.at[k]).start()
        for f in range(FRAMES):
            here = pl.ds(f * NFFT + k * CHUNK, CHUNK)
            pltpu.make_async_copy(
                v_hbm.at[:, :, here], v_buf.at[:, :, here], chunk_sem.at[k]
            ).start()

    def chunk_wait(k):
        table_part = w_buf.at[:, pl.ds(0, CHUNK)]
        pltpu.make_async_copy(table_part, table_part, chunk_sem.at[k]).wait()
        frames_part = v_buf.at[:, :, pl.ds(0, FRAMES * CHUNK)]
        pltpu.make_async_copy(frames_part, frames_part, chunk_sem.at[k]).wait()

    barrier = pltpu.get_barrier_semaphore()

    def greet(k, carry):
        other = lax.rem(me + k, DEVICES)
        where = (lax.div(other, BLOCKS), lax.rem(other, BLOCKS))
        pl.semaphore_signal(barrier, inc=1, device_id=where, device_id_type=MESH)
        return carry

    lax.fori_loop(1, DEVICES, greet, 0, unroll=5)
    proto_copy.wait()

    def filter_chunk(k, slot, first, last):
        for tile in range(CHUNK // LANES):
            offset = k * CHUNK + tile * LANES
            offset = offset if isinstance(offset, int) else pl.multiple_of(offset, LANES)
            taps = [proto_ref[pl.ds(t, 1), pl.ds(offset, LANES)] for t in range(TAPS)]
            lanes = pl.ds(tile * LANES, LANES)
            for part in range(2):
                window = {}
                for s in range(first, last):
                    value = None
                    for t in range(TAPS):
                        f = s + t - EDGE
                        if 0 <= f < FRAMES:
                            if f not in window:
                                at = f * NFFT + offset
                                at = at if isinstance(at, int) else pl.multiple_of(at, LANES)
                                window[f] = v_buf[part, :, pl.ds(at, LANES)].astype(jnp.float32)
                            term = taps[t] * window[f]
                            value = term if value is None else value + term
                    group, place = (s - first) // QUAD, (s - first) % QUAD
                    row = (group * 2 + part) * QUAD_ROWS + place * INPUTS
                    if value is None:
                        value = jnp.zeros((INPUTS, LANES), jnp.float32)
                    slot[pl.ds(row, INPUTS), lanes] = value.astype(jnp.bfloat16)

    def product(k, slot, rows):
        offset = k * CHUNK
        offset = offset if isinstance(offset, int) else pl.multiple_of(offset, CHUNK)
        return lax.dot_general(
            w_buf[:, pl.ds(offset, CHUNK)],
            slot[pl.ds(0, rows), :],
            CONTRACT,
            preferred_element_type=jnp.float32,
        )

    lane = lax.broadcasted_iota(jnp.int32, (BAND, LANES), 1)

    def combined(column):
        lanes = pl.ds(column * LANES, LANES)
        turned = pltpu.roll(total[pl.ds(BAND, BAND), lanes], QUAD_ROWS, 1)
        return total[pl.ds(0, BAND), lanes] + jnp.where(lane < QUAD_ROWS, -turned, turned)

    late_rows = 4 * 2 * QUAD_ROWS
    chunk_wait(0)
    filter_chunk(0, slots[0], QUAD, FRAMES + QUAD)
    for k in range(CHUNKS):
        if k + 1 < CHUNKS:
            chunk_wait(k + 1)
            filter_chunk(k + 1, slots[(k + 1) % 2], QUAD, FRAMES + QUAD)
        added = product(k, slots[k % 2], late_rows)
        if k == 0:
            total[...] = added
        else:
            total[...] += added

    for column in range(4):
        rows_buf[pl.ds(column, BAND, stride=4), :] = combined(column)
    late_send[...] = rows_buf[...].reshape(BAND, 4, LANES).astype(jnp.bfloat16)

    pl.semaphore_wait(barrier, DEVICES - 1)
    partners = Partners()

    def send(found, source, target, send_sem, recv_sem):
        for where in found:
            pltpu.make_async_remote_copy(
                src_ref=source.at[where[0] * BLOCKS + where[1]],
                dst_ref=target.at[me],
                send_sem=send_sem,
                recv_sem=recv_sem,
                device_id=where,
                device_id_type=MESH,
            ).start()

    def send_late(step):
        send(partners.layer(step), late_send, late_out, late_send_sem, late_recv_sem)

    def send_early(step):
        send(partners.layer(step), early_send, early_out, early_send_sem, early_recv_sem)

    early_rows = 2 * QUAD_ROWS
    for k in range(CHUNKS):
        send_late(k)
        filter_chunk(k, slots[k % 2], 0, QUAD)
        added = product(k, slots[k % 2], early_rows)
        if k == 0:
            total[:, pl.ds(0, LANES)] = added
        else:
            total[:, pl.ds(0, LANES)] += added
    early_send[...] = combined(0).reshape(BAND, 1, LANES)

    def early_layer(step, carry):
        send_early(step)
        return carry

    lax.fori_loop(0, 7, early_layer, 0)
    send_early(7)
    own = [
        pltpu.make_async_copy(late_send.at[me], late_out.at[me], late_recv_sem),
        pltpu.make_async_copy(early_send.at[me], early_out.at[me], early_recv_sem),
    ]
    for copy in own:
        copy.start()

    for buffer, sem in ((late_send, late_send_sem), (early_send, early_send_sem)):
        sent = buffer.at[pl.ds(0, DEVICES - 1)]
        pltpu.make_async_copy(sent, sent, sem).wait()
    pltpu.make_async_copy(late_out, late_out, late_recv_sem).wait()
    pltpu.make_async_copy(early_out, early_out, early_recv_sem).wait()


def exchange(voltages, prototype, table):
    return pl.pallas_call(
        exchange_kernel,
        out_shape=(
            jax.ShapeDtypeStruct((DEVICES, 4, LANES), jnp.bfloat16),
            jax.ShapeDtypeStruct((DEVICES, 1, LANES), jnp.float32),
        ),
        in_specs=[pl.BlockSpec(memory_space=pltpu.HBM)] * 3,
        out_specs=(pl.BlockSpec(memory_space=pl.ANY),) * 2,
        scratch_shapes=[
            pltpu.VMEM((TAPS, NFFT), jnp.float32),
            pltpu.VMEM((2, INPUTS, FRAMES * NFFT), jnp.bfloat16),
            pltpu.VMEM((2 * BAND, NFFT), jnp.bfloat16),
            pltpu.VMEM((8 * QUAD_ROWS, CHUNK), jnp.bfloat16),
            pltpu.VMEM((8 * QUAD_ROWS, CHUNK), jnp.bfloat16),
            pltpu.VMEM((2 * BAND, 4 * LANES), jnp.float32),
            pltpu.VMEM((4 * BAND, LANES), jnp.float32),
            pltpu.VMEM((DEVICES, 4, LANES), jnp.bfloat16),
            pltpu.VMEM((DEVICES, 1, LANES), jnp.float32),
            pltpu.SemaphoreType.DMA,
            pltpu.SemaphoreType.DMA((CHUNKS,)),
            pltpu.SemaphoreType.DMA,
            pltpu.SemaphoreType.DMA,
            pltpu.SemaphoreType.DMA,
            pltpu.SemaphoreType.DMA,
        ],
        compiler_params=pltpu.CompilerParams(
            collective_id=0, has_side_effects=True, vmem_limit_bytes=32 * 1024 * 1024
        ),
        name="channelize_and_send",
    )(voltages, prototype, table)


def correlate_kernel(late_ref, early_ref, out_hbm, late, early, gathered, right, out_buf, out_sem):
    late[...] = late_ref[...].astype(jnp.float32).reshape(DEVICES * 4, LANES)
    early[...] = early_ref[...].reshape(DEVICES, LANES)
    lane = lax.broadcasted_iota(jnp.int32, (8, LANES), 1)
    row = lax.broadcasted_iota(jnp.int32, (8, LANES), 0)
    source = lax.rem(lane // INPUTS - row + 8, 8)
    back = lax.rem(lane + row * INPUTS, LANES)
    for group in range(8):
        columns = pl.ds(group * LANES, LANES)
        for block in range(BLOCKS):
            for quad in range(4):
                if quad > 0:
                    tile = late[pl.ds(group * 128 + block * 4 + quad - 1, 8, stride=16), :]
                else:
                    tile = early[pl.ds(group * 32 + block, 8, stride=4), :]
                    if block > 0:
                        tile = tile + late[pl.ds(group * 128 + block * 4 - 1, 8, stride=16), :]
                tile = pltpu.roll(tile, 0, 1, stride=INPUTS, stride_axis=0)
                tile = jnp.take_along_axis(tile, source, axis=0)
                tile = jnp.take_along_axis(tile, back, axis=1)
                at = (block * 4 + quad) * QUAD
                gathered[pl.ds(at, QUAD), columns] = tile[:QUAD]
                gathered[pl.ds(64 + at, QUAD), columns] = tile[QUAD:]
    right[...] = gathered[...].astype(jnp.bfloat16)

    wide = lax.broadcasted_iota(jnp.int32, (LANES, LANES), 1)
    copies = []
    for group in range(8):
        columns = pl.ds(group * LANES, LANES)
        square = gathered[:, columns].T
        other = pltpu.roll(square, 64, 1)
        other = jnp.where(wide < 64, other, -other)
        for part, left in enumerate((square, other)):
            product = jnp.dot(
                left.astype(jnp.bfloat16), right[...], preferred_element_type=jnp.float32
            )
            out_buf[0, part, columns, :] = (product * (1.0 / 64.0)).astype(jnp.bfloat16)
        copies.append(
            pltpu.make_async_copy(
                out_buf.at[:, :, columns, :], out_hbm.at[:, :, columns, :], out_sem.at[group]
            )
        )
        copies[-1].start()
    for copy in copies:
        copy.wait()


def correlate(late, early):
    everyone = STATIONS * INPUTS
    shape = (1, 2, everyone, everyone)
    return pl.pallas_call(
        correlate_kernel,
        out_shape=jax.ShapeDtypeStruct(shape, jnp.bfloat16),
        in_specs=[pl.BlockSpec(memory_space=pltpu.VMEM)] * 2,
        out_specs=pl.BlockSpec(memory_space=pltpu.HBM),
        scratch_shapes=[
            pltpu.VMEM((DEVICES * 4, LANES), jnp.float32),
            pltpu.VMEM((DEVICES, LANES), jnp.float32),
            pltpu.VMEM((LANES, everyone), jnp.float32),
            pltpu.VMEM((LANES, everyone), jnp.bfloat16),
            pltpu.VMEM(shape, jnp.bfloat16),
            pltpu.SemaphoreType.DMA((8,)),
        ],
        compiler_params=pltpu.CompilerParams(vmem_limit_bytes=32 * 1024 * 1024),
        name="correlate",
    )(late, early)


def local(voltages, prototype):
    table = jnp.asarray(channel_table())
    held = [pltpu.with_memory_space_constraint(x, pltpu.HBM) for x in (voltages, prototype, table)]
    return correlate(*exchange(*held))


def solution(mesh):
    return jax.shard_map(
        local,
        mesh=mesh,
        in_specs=(P(None, "station", "tblock"), P()),
        out_specs=P(("station", "tblock"), None, None, None),
        check_vma=False,
    )
```

time: 40.3 us -> 33.1 us (0.82)
  local copies, waits for them, and re-layouts: 5.21 us -> 0 us
  Pallas kernels: 34.9 us -> 33 us
    unnamed x6 -> x0, local copies, waits for them, and re-layouts: 5.21 us -> none
    pallas_call x2, Pallas kernels: 34.9 us -> 33 us  [the longest x1 30.1 us: exchange(): pl.pallas_call(exchange_kernel, out_shape=(jax.ShapeDtypeStruct((DEVICES,...]
where the time goes in v2:
time: 33.1 us; the launch traced here: 33 us
  Pallas kernels  33 us (100%)
    pallas_call x1, Pallas kernels, exchange(): pl.pallas_call(exchange_kernel, out_shape=(jax.ShapeDtypeStruct((DEVICES,...  30.1 us
    pallas_call x1, Pallas kernels, correlate(): pl.pallas_call(correlate_kernel, out_shape=jax.ShapeDtypeStruct(shape, jn...  2.89 us

profile of v2, /device:TPU:1, one launch (start us, length us, event | category | flops | bytes accessed | tf_op | source)
XLA Modules:
  0.0 33.0 jit_solution(3588296457487663753)
XLA Ops:
  0.0 30.1 %channelize_and_send.1 = (bf16[256,4,128]{2,1,0:T(4,128)(2,1)S(1)}, f32[256,1,128]{2,1,0:T(1,128)S(1)}) custom-call(bf16[2,16,65536]{2,1,0:T(8,128)(2,1)} %v_hbm.1, f32[4,4096]{1,0:T(4,128)} %proto_hbm.1, bf16[512,4096]{1,0:T(8,128)(2,1)} %constant.2.clone.w_hbm), custom_call_target="tpu_custom_call" | custom-call | tf_op jit(solution)/shard_map/channelize_and_send/pallas_call | solution.py:254
  30.2 2.9 %correlate.1 = bf16[1,2,1024,1024]{3,2,1,0:T(8,128)(2,1)} custom-call(bf16[256,4,128]{2,1,0:T(4,128)(2,1)S(1)} %get-tuple-element.7.late_ref, f32[256,1,128]{2,1,0:T(1,128)S(1)} %get-tuple-element.8.early_ref), custom_call_target="tpu_custom_call" | custom-call | tf_op jit(solution)/shard_map/correlate/pallas_call | solution.py:336

commit v3 on v2

v3 whole, which is shorter than its diff:
```python
import math

import jax
import jax.numpy as jnp
import ml_dtypes
import numpy as np
from jax import lax
from jax.experimental import pallas as pl
from jax.experimental.pallas import tpu as pltpu
from jax.sharding import PartitionSpec as P

ROOT = 64
NFFT = 4096
TAPS = 4
BAND = 256
FRAMES = 16
INPUTS = 16
EDGE = TAPS - 1
QUAD = 4
QUAD_ROWS = QUAD * INPUTS
STATIONS = 64
BLOCKS = 4
DEVICES = STATIONS * BLOCKS
LANES = 128
HALF = NFFT // 2
PAIRS = BAND // 2
CHUNK = 512
CHUNKS = HALF // CHUNK
GROUPS = FRAMES // QUAD + 1
TILES = CHUNK // LANES
MESH = pl.DeviceIdType.MESH
CONTRACT = (((1,), (1,)), ((), ()))


def channel_table():
    def angles(first, second, period):
        product = (first[:, None] * second[None, :]) % period
        return product.astype(np.float32) * np.float32(2.0 * math.pi / period)

    def rounded(values):
        return values.astype(ml_dtypes.bfloat16).astype(np.float64)

    digits = np.arange(ROOT)
    first = angles(digits, digits, ROOT)
    root = rounded(np.cos(first)) - 1j * rounded(np.sin(first))
    twist_angle = angles(digits, digits, NFFT)
    twist = np.cos(twist_angle).astype(np.float64) - 1j * np.sin(twist_angle).astype(np.float64)
    high = (NFFT - BAND) // 2 // ROOT + np.arange(BAND // ROOT)
    table = (
        root.T[None, :, :, None] * twist.T[None, :, None, :] * root[:, high].T[:, None, None, :]
    )
    table = table.reshape(BAND // 2, 2, NFFT)[:, :, : NFFT // 2] / (32.0 * ROOT)
    table = np.swapaxes(table, 0, 1)
    table = np.concatenate([table.real, table.imag], axis=1)
    return table.astype(np.float32).astype(ml_dtypes.bfloat16)


def far_first(step, size):
    return size // 2 + (1 - 2 * (step % 2)) * ((step + 1) // 2)


class Partners:
    def __init__(self):
        station = lax.axis_index("station")
        block = lax.axis_index("tblock")
        self.z = lax.rem(station, 8)
        x = lax.div(block, 2) * 2 + lax.rem(lax.div(station, 8), 2)
        y = lax.div(station, 16)
        core = lax.rem(block, 2)
        xs, ys = {}, {}
        for d in range(4):
            there = lax.rem(x + d, 4)
            xs[d] = (lax.rem(there, 2) * 8, lax.div(there, 2) * 2)
            ys[d] = lax.rem(y + d, 4) * 16
        offsets = [(dx, dy, dc) for dx in range(4) for dy in range(4) for dc in (1, 0)]
        offsets.sort(key=lambda o: -(min(o[0], 4 - o[0]) + min(o[1], 4 - o[1])))
        self.plane = []
        for dx, dy, dc in offsets:
            low, high = xs[dx]
            self.plane.append((ys[dy] + low, high + (core if dc == 0 else 1 - core)))

    def layer(self, step):
        if isinstance(step, int):
            shift = far_first(step, 8)
        else:
            odd = lax.rem(step, 2)
            shift = 4 + (1 - 2 * odd) * lax.div(step + 1, 2)
        z = lax.rem(self.z + shift, 8)
        found = [(base + z, block) for base, block in self.plane]
        return found[:-1] if isinstance(step, int) and step == 7 else found


def exchange_kernel(
    v_hbm,
    proto_hbm,
    w_hbm,
    moved,
    proto_ref,
    v_buf,
    w_buf,
    sums,
    differences,
    first_quad,
    rows_buf,
    edge_out,
    edge_in,
    leaving,
    proto_sem,
    chunk_sem,
    w_sem,
    edge_send,
    edge_recv,
    send_sem,
    recv_sem,
):
    station = lax.axis_index("station")
    block = lax.axis_index("tblock")
    me = station * BLOCKS + block
    partners = Partners()
    barrier = pltpu.get_barrier_semaphore()

    def greet(step, part):
        for where in partners.layer(step)[part * 16 : part * 16 + 16]:
            pl.semaphore_signal(barrier, inc=1, device_id=where, device_id_type=MESH)

    def load(k, frames):
        for f in frames:
            for half in range(2):
                at = f * NFFT + half * HALF + k * CHUNK
                here = pl.ds(at if isinstance(f, int) else pl.multiple_of(at, CHUNK), CHUNK)
                pltpu.make_async_copy(
                    v_hbm.at[:, :, here], v_buf.at[:, :, here], chunk_sem.at[k]
                ).start()

    proto_copy = pltpu.make_async_copy(proto_hbm, proto_ref, proto_sem)
    proto_copy.start()
    greet(0, 0)
    load(0, range(FRAMES))
    greet(0, 1)
    load(1, range(FRAMES))
    w_copy = pltpu.make_async_copy(w_hbm, w_buf, w_sem)
    proto_copy.wait()

    def filter_tile(offset):
        spots = [pl.multiple_of(offset + half * HALF, LANES) for half in range(2)]
        taps = [
            [proto_ref[pl.ds(t, 1), pl.ds(spot, LANES)] for t in range(TAPS)] for spot in spots
        ]
        lanes = pl.ds(spots[0], LANES)
        for part in range(2):
            window = {}
            for s in range(FRAMES + EDGE):
                values = []
                for half in range(2):
                    value = None
                    for t in range(TAPS):
                        f = s + t - EDGE
                        if 0 <= f < FRAMES:
                            if (half, f) not in window:
                                at = pl.ds(pl.multiple_of(f * NFFT + spots[half], LANES), LANES)
                                window[half, f] = v_buf[part, :, at].astype(jnp.float32)
                            term = taps[half][t] * window[half, f]
                            value = term if value is None else value + term
                    values.append(value)
                row = (s // QUAD * 2 + part) * QUAD_ROWS + s % QUAD * INPUTS
                rows = pl.ds(row, INPUTS)
                sums[rows, lanes] = (values[0] + values[1]).astype(jnp.bfloat16)
                differences[rows, lanes] = (values[0] - values[1]).astype(jnp.bfloat16)

    for part in range(2):
        rows = pl.ds((2 * GROUPS - 2 + part) * QUAD_ROWS + EDGE * INPUTS, INPUTS)
        sums[rows, :] = jnp.zeros((INPUTS, HALF), jnp.bfloat16)
        differences[rows, :] = jnp.zeros((INPUTS, HALF), jnp.bfloat16)

    for k in range(CHUNKS):
        chunk = v_buf.at[:, :, pl.ds(0, 2 * FRAMES * CHUNK)]
        pltpu.make_async_copy(chunk, chunk, chunk_sem.at[k]).wait()
        turns = TILES // 2

        def two_tiles(turn, carry):
            for part in range(2):
                if not isinstance(turn, int) or k * turns + turn < 7:
                    greet(k * turns + turn + 1, part)
                if k + 2 < CHUNKS:
                    share = FRAMES // TILES
                    load(k + 2, [(turn * 2 + part) * share + f for f in range(share)])
                filter_tile(k * CHUNK + (turn * 2 + part) * LANES)
            return carry

        if k < CHUNKS - 1:
            lax.fori_loop(0, turns, two_tiles, 0)
        else:
            for turn in range(turns):
                two_tiles(turn, 0)
        if k == 1:
            w_copy.start()

    w_copy.wait()
    lane = lax.broadcasted_iota(jnp.int32, (PAIRS, LANES), 1)
    for parity, operand in enumerate((sums, differences)):
        total = lax.dot_general(
            w_buf[parity], operand[...], CONTRACT, preferred_element_type=jnp.float32
        )
        for group in range(GROUPS):
            own = total[:, group * LANES : (group + 1) * LANES]
            turned = pltpu.roll(own[PAIRS:], QUAD_ROWS, 1)
            value = own[:PAIRS] + jnp.where(lane < QUAD_ROWS, -turned, turned)
            if group == 0:
                first_quad[parity] = value
            elif group == GROUPS - 1:
                edge_out[parity] = value.astype(jnp.bfloat16)
            else:
                at = group // 2 * 2 * BAND + parity * 2 + group % 2
                rows_buf[pl.ds(at, PAIRS, stride=4), :] = value
    late = rows_buf[pl.ds(2 * BAND, 2 * BAND), :].reshape(BAND, 2, LANES)
    leaving[1] = late.astype(jnp.bfloat16)

    edge_copy = pltpu.make_async_remote_copy(
        src_ref=edge_out,
        dst_ref=edge_in,
        send_sem=edge_send,
        recv_sem=edge_recv,
        device_id=(station, lax.min(block + 1, BLOCKS - 1)),
        device_id_type=MESH,
    )

    @pl.when(block == 0)
    def _():
        edge_in[...] = jnp.zeros_like(edge_in)

    pl.semaphore_wait(barrier, DEVICES - 1)

    @pl.when(block < BLOCKS - 1)
    def _():
        edge_copy.start()

    def send(step, half):
        for where in partners.layer(step):
            pltpu.make_async_remote_copy(
                src_ref=leaving.at[half, where[0] * BLOCKS + where[1]],
                dst_ref=moved.at[half, me],
                send_sem=send_sem,
                recv_sem=recv_sem,
                device_id=where,
                device_id_type=MESH,
            ).start()

    def send_half(half):
        def layer(step, carry):
            send(step, half)
            return carry

        lax.fori_loop(0, 7, layer, 0)
        send(7, half)
        pltpu.make_async_copy(leaving.at[half, me], moved.at[half, me], recv_sem).start()

    send_half(1)

    @pl.when(block > 0)
    def _():
        edge_copy.wait_recv()

    for parity in range(2):
        value = first_quad[parity] + edge_in[parity].astype(jnp.float32)
        rows_buf[pl.ds(parity * 2, PAIRS, stride=4), :] = value
    early = rows_buf[pl.ds(0, 2 * BAND), :].reshape(BAND, 2, LANES)
    leaving[0] = early.astype(jnp.bfloat16)
    send_half(0)

    @pl.when(block < BLOCKS - 1)
    def _():
        edge_copy.wait_send()

    sent = leaving.at[:, pl.ds(0, DEVICES - 1)]
    pltpu.make_async_copy(sent, sent, send_sem).wait()
    pltpu.make_async_copy(moved, moved, recv_sem).wait()


def exchange(voltages, prototype, table):
    operands = (voltages, prototype, table)
    return pl.pallas_call(
        exchange_kernel,
        out_shape=jax.ShapeDtypeStruct((2, DEVICES, 2, LANES), jnp.bfloat16),
        in_specs=[pl.BlockSpec(memory_space=pltpu.HBM)] * 3,
        out_specs=pl.BlockSpec(memory_space=pl.ANY),
        scratch_shapes=[
            pltpu.VMEM((TAPS, NFFT), jnp.float32),
            pltpu.VMEM((2, INPUTS, FRAMES * NFFT), jnp.bfloat16),
            pltpu.VMEM((2, BAND, HALF), jnp.bfloat16),
            pltpu.VMEM((GROUPS * LANES, HALF), jnp.bfloat16),
            pltpu.VMEM((GROUPS * LANES, HALF), jnp.bfloat16),
            pltpu.VMEM((2, PAIRS, LANES), jnp.float32),
            pltpu.VMEM((4 * BAND, LANES), jnp.float32),
            pltpu.VMEM((2, PAIRS, LANES), jnp.bfloat16),
            pltpu.VMEM((2, PAIRS, LANES), jnp.bfloat16),
            pltpu.VMEM((2, DEVICES, 2, LANES), jnp.bfloat16),
            pltpu.SemaphoreType.DMA,
            pltpu.SemaphoreType.DMA((CHUNKS,)),
            pltpu.SemaphoreType.DMA,
            pltpu.SemaphoreType.DMA,
            pltpu.SemaphoreType.DMA,
            pltpu.SemaphoreType.DMA,
            pltpu.SemaphoreType.DMA,
        ],
        compiler_params=pltpu.CompilerParams(
            collective_id=0, has_side_effects=True, vmem_limit_bytes=32 * 1024 * 1024
        ),
        name="channelize_and_send",
    )(*[pltpu.with_memory_space_constraint(operand, pltpu.HBM) for operand in operands])


def correlate_kernel(moved_ref, out_hbm, moved, gathered, right, out_buf, out_sem):
    for half in range(2):
        rows = moved_ref[half].astype(jnp.float32).reshape(DEVICES * 2, LANES)
        moved[pl.ds(half * DEVICES * 2, DEVICES * 2), :] = rows
    lane = lax.broadcasted_iota(jnp.int32, (8, LANES), 1)
    row = lax.broadcasted_iota(jnp.int32, (8, LANES), 0)
    source = lax.rem(lane // INPUTS - row + 8, 8)
    back = lax.rem(lane + row * INPUTS, LANES)
    for group in range(8):
        columns = pl.ds(group * LANES, LANES)
        for block in range(BLOCKS):
            for quad in range(4):
                first = quad // 2 * DEVICES * 2 + group * 64 + block * 2 + quad % 2
                tile = moved[pl.ds(first, 8, stride=8), :]
                tile = pltpu.roll(tile, 0, 1, stride=INPUTS, stride_axis=0)
                tile = jnp.take_along_axis(tile, source, axis=0)
                tile = jnp.take_along_axis(tile, back, axis=1)
                at = (block * 4 + quad) * QUAD
                gathered[pl.ds(at, QUAD), columns] = tile[:QUAD]
                gathered[pl.ds(64 + at, QUAD), columns] = tile[QUAD:]
    right[...] = gathered[...].astype(jnp.bfloat16)

    wide = lax.broadcasted_iota(jnp.int32, (LANES, LANES), 1)
    copies = []
    for group in range(8):
        columns = pl.ds(group * LANES, LANES)
        square = gathered[:, columns].T
        other = pltpu.roll(square, 64, 1)
        other = jnp.where(wide < 64, other, -other)
        for part, left in enumerate((square, other)):
            product = jnp.dot(
                left.astype(jnp.bfloat16), right[...], preferred_element_type=jnp.float32
            )
            out_buf[0, part, columns, :] = (product * (1.0 / 64.0)).astype(jnp.bfloat16)
        copies.append(
            pltpu.make_async_copy(
                out_buf.at[:, :, columns, :], out_hbm.at[:, :, columns, :], out_sem.at[group]
            )
        )
        copies[-1].start()
    for copy in copies:
        copy.wait()


def correlate(moved):
    everyone = STATIONS * INPUTS
    shape = (1, 2, everyone, everyone)
    return pl.pallas_call(
        correlate_kernel,
        out_shape=jax.ShapeDtypeStruct(shape, jnp.bfloat16),
        in_specs=[pl.BlockSpec(memory_space=pltpu.VMEM)],
        out_specs=pl.BlockSpec(memory_space=pltpu.HBM),
        scratch_shapes=[
            pltpu.VMEM((DEVICES * 4, LANES), jnp.float32),
            pltpu.VMEM((LANES, everyone), jnp.float32),
            pltpu.VMEM((LANES, everyone), jnp.bfloat16),
            pltpu.VMEM(shape, jnp.bfloat16),
            pltpu.SemaphoreType.DMA((8,)),
        ],
        compiler_params=pltpu.CompilerParams(vmem_limit_bytes=32 * 1024 * 1024),
        name="correlate",
    )(moved)


def local(voltages, prototype):
    table = jnp.asarray(channel_table())
    return correlate(exchange(voltages, prototype, table))


def solution(mesh):
    return jax.shard_map(
        local,
        mesh=mesh,
        in_specs=(P(None, "station", "tblock"), P()),
        out_specs=P(("station", "tblock"), None, None, None),
        check_vma=False,
    )
```

time: 33.1 us -> 29.6 us (0.89)
  Pallas kernels: 33 us -> 29.4 us
    pallas_call x1, Pallas kernels: 30.1 us -> 26.5 us  [exchange(): pl.pallas_call(exchange_kernel, out_shape=jax.ShapeDtypeStruct((2, DEVICE...]
where the time goes in v3:
time: 29.6 us; the launch traced here: 29.4 us
  Pallas kernels  29.4 us (99%)
    pallas_call x1, Pallas kernels, exchange(): pl.pallas_call(exchange_kernel, out_shape=jax.ShapeDtypeStruct((2, DEVICE...  26.5 us
    pallas_call x1, Pallas kernels, correlate(): pl.pallas_call(correlate_kernel, out_shape=jax.ShapeDtypeStruct(shape, jn...  2.91 us

profile of v3, /device:TPU:1, one launch (start us, length us, event | category | flops | bytes accessed | tf_op | source)
XLA Modules:
  0.0 29.4 jit_solution(15999366432617600247)
XLA Ops:
  0.0 26.5 %channelize_and_send.1.moved_ref = bf16[2,256,2,128]{3,2,1,0:T(2,128)(2,1)S(1)} custom-call(bf16[2,16,65536]{2,1,0:T(8,128)(2,1)} %v_hbm.1, f32[4,4096]{1,0:T(4,128)} %proto_hbm.1, bf16[2,256,2048]{2,1,0:T(8,128)(2,1)} %constant.2.clone.w_hbm), custom_call_target="tpu_custom_call" | custom-call | tf_op jit(solution)/shard_map/channelize_and_send/pallas_call | solution.py:281
  26.5 2.9 %correlate.1 = bf16[1,2,1024,1024]{3,2,1,0:T(8,128)(2,1)} custom-call(bf16[2,256,2,128]{3,2,1,0:T(2,128)(2,1)S(1)} %channelize_and_send.1.moved_ref), custom_call_target="tpu_custom_call" | custom-call | tf_op jit(solution)/shard_map/correlate/pallas_call | solution.py:359

commit v4 on v3

--- a/solution.py
+++ b/solution.py
@@ -28,6 +28,7 @@
 CHUNKS = HALF // CHUNK
 GROUPS = FRAMES // QUAD + 1
 TILES = CHUNK // LANES
+GREETED = 5
 MESH = pl.DeviceIdType.MESH
 CONTRACT = (((1,), (1,)), ((), ()))
 
@@ -134,10 +135,11 @@
 
     proto_copy = pltpu.make_async_copy(proto_hbm, proto_ref, proto_sem)
     proto_copy.start()
-    greet(0, 0)
-    load(0, range(FRAMES))
-    greet(0, 1)
-    load(1, range(FRAMES))
+    for step in range(GREETED):
+        greet(step, 0)
+        greet(step, 1)
+        if step < 2:
+            load(step, range(FRAMES))
     w_copy = pltpu.make_async_copy(w_hbm, w_buf, w_sem)
     proto_copy.wait()
 
@@ -178,40 +180,47 @@
         turns = TILES // 2
 
         def two_tiles(turn, carry):
+            step = GREETED + k * turns + turn
             for part in range(2):
-                if not isinstance(turn, int) or k * turns + turn < 7:
-                    greet(k * turns + turn + 1, part)
+                if k == 0 or (k == 1 and turn == 0):
+                    greet(step, part)
                 if k + 2 < CHUNKS:
                     share = FRAMES // TILES
                     load(k + 2, [(turn * 2 + part) * share + f for f in range(share)])
                 filter_tile(k * CHUNK + (turn * 2 + part) * LANES)
             return carry
 
-        if k < CHUNKS - 1:
-            lax.fori_loop(0, turns, two_tiles, 0)
-        else:
+        if k == 1:
             for turn in range(turns):
                 two_tiles(turn, 0)
+        else:
+            lax.fori_loop(0, turns, two_tiles, 0)
         if k == 1:
             w_copy.start()
 
     w_copy.wait()
     lane = lax.broadcasted_iota(jnp.int32, (PAIRS, LANES), 1)
-    for parity, operand in enumerate((sums, differences)):
-        total = lax.dot_general(
-            w_buf[parity], operand[...], CONTRACT, preferred_element_type=jnp.float32
-        )
-        for group in range(GROUPS):
-            own = total[:, group * LANES : (group + 1) * LANES]
-            turned = pltpu.roll(own[PAIRS:], QUAD_ROWS, 1)
-            value = own[:PAIRS] + jnp.where(lane < QUAD_ROWS, -turned, turned)
-            if group == 0:
-                first_quad[parity] = value
-            elif group == GROUPS - 1:
-                edge_out[parity] = value.astype(jnp.bfloat16)
-            else:
-                at = group // 2 * 2 * BAND + parity * 2 + group % 2
-                rows_buf[pl.ds(at, PAIRS, stride=4), :] = value
+    def transform(first, last):
+        for parity, operand in enumerate((sums, differences)):
+            total = lax.dot_general(
+                w_buf[parity],
+                operand[pl.ds(first * LANES, (last - first) * LANES), :],
+                CONTRACT,
+                preferred_element_type=jnp.float32,
+            )
+            for group in range(first, last):
+                own = total[:, (group - first) * LANES : (group - first + 1) * LANES]
+                turned = pltpu.roll(own[PAIRS:], QUAD_ROWS, 1)
+                value = own[:PAIRS] + jnp.where(lane < QUAD_ROWS, -turned, turned)
+                if group == 0:
+                    first_quad[parity] = value
+                elif group == GROUPS - 1:
+                    edge_out[parity] = value.astype(jnp.bfloat16)
+                else:
+                    at = group // 2 * 2 * BAND + parity * 2 + group % 2
+                    rows_buf[pl.ds(at, PAIRS, stride=4), :] = value
+
+    transform(2, GROUPS)
     late = rows_buf[pl.ds(2 * BAND, 2 * BAND), :].reshape(BAND, 2, LANES)
     leaving[1] = late.astype(jnp.bfloat16)
 
@@ -245,16 +254,23 @@
                 device_id_type=MESH,
             ).start()
 
-    def send_half(half):
-        def layer(step, carry):
+    def send_planes(half, first, last):
+        def plane(step, carry):
             send(step, half)
             return carry
 
-        lax.fori_loop(0, 7, layer, 0)
-        send(7, half)
-        pltpu.make_async_copy(leaving.at[half, me], moved.at[half, me], recv_sem).start()
-
-    send_half(1)
+        if first < 7:
+            lax.fori_loop(first, min(last, 7), plane, 0)
+        if last == 8:
+            send(7, half)
+
+    far = 4
+    send_planes(1, 0, far)
+    transform(0, 2)
+
+    @pl.when(block == 2)
+    def _():
+        send_planes(1, far, 8)
 
     @pl.when(block > 0)
     def _():
@@ -265,7 +281,15 @@
         rows_buf[pl.ds(parity * 2, PAIRS, stride=4), :] = value
     early = rows_buf[pl.ds(0, 2 * BAND), :].reshape(BAND, 2, LANES)
     leaving[0] = early.astype(jnp.bfloat16)
-    send_half(0)
+    send_planes(0, 0, far)
+
+    @pl.when(block != 2)
+    def _():
+        send_planes(1, far, 8)
+
+    send_planes(0, far, 8)
+    for half in range(2):
+        pltpu.make_async_copy(leaving.at[half, me], moved.at[half, me], recv_sem).start()
 
     @pl.when(block < BLOCKS - 1)
     def _():

time: 29.6 us -> 28.4 us (0.959)
  Pallas kernels: 29.4 us -> 28.3 us
    pallas_call x1, Pallas kernels: 26.5 us -> 25.4 us  [exchange(): pl.pallas_call(exchange_kernel, out_shape=jax.ShapeDtypeStruct((2, DEVICE...]
where the time goes in v4:
time: 28.4 us; the launch traced here: 28.3 us
  Pallas kernels  28.3 us (100%)
    pallas_call x1, Pallas kernels, exchange(): pl.pallas_call(exchange_kernel, out_shape=jax.ShapeDtypeStruct((2, DEVICE...  25.4 us
    pallas_call x1, Pallas kernels, correlate(): pl.pallas_call(correlate_kernel, out_shape=jax.ShapeDtypeStruct(shape, jn...  2.9 us

profile of v4, /device:TPU:1, one launch (start us, length us, event | category | flops | bytes accessed | tf_op | source)
XLA Modules:
  0.0 28.3 jit_solution(3469105083250739980)
XLA Ops:
  0.0 25.4 %channelize_and_send.1.moved_ref = bf16[2,256,2,128]{3,2,1,0:T(2,128)(2,1)S(1)} custom-call(bf16[2,16,65536]{2,1,0:T(8,128)(2,1)} %v_hbm.1, f32[4,4096]{1,0:T(4,128)} %proto_hbm.1, bf16[2,256,2048]{2,1,0:T(8,128)(2,1)} %constant.2.clone.w_hbm), custom_call_target="tpu_custom_call" | custom-call | tf_op jit(solution)/shard_map/channelize_and_send/pallas_call | solution.py:305
  25.4 2.9 %correlate.1 = bf16[1,2,1024,1024]{3,2,1,0:T(8,128)(2,1)} custom-call(bf16[2,256,2,128]{3,2,1,0:T(2,128)(2,1)S(1)} %channelize_and_send.1.moved_ref), custom_call_target="tpu_custom_call" | custom-call | tf_op jit(solution)/shard_map/correlate/pallas_call | solution.py:383

commit v5 on v4

--- a/solution.py
+++ b/solution.py
@@ -28,7 +28,8 @@
 CHUNKS = HALF // CHUNK
 GROUPS = FRAMES // QUAD + 1
 TILES = CHUNK // LANES
-GREETED = 5
+FAR = ((0, 0, 5), (1, 0, 3))
+NEAR = ((0, 5, 7), (1, 3, 5), (0, 7, 8), (1, 5, 7), (1, 7, 8))
 MESH = pl.DeviceIdType.MESH
 CONTRACT = (((1,), (1,)), ((), ()))
 
@@ -80,15 +81,15 @@
             low, high = xs[dx]
             self.plane.append((ys[dy] + low, high + (core if dc == 0 else 1 - core)))
 
-    def layer(self, step):
+    def half_plane(self, step, part):
         if isinstance(step, int):
             shift = far_first(step, 8)
         else:
             odd = lax.rem(step, 2)
             shift = 4 + (1 - 2 * odd) * lax.div(step + 1, 2)
         z = lax.rem(self.z + shift, 8)
-        found = [(base + z, block) for base, block in self.plane]
-        return found[:-1] if isinstance(step, int) and step == 7 else found
+        found = [(base + z, block) for base, block in self.plane[part * 16 : part * 16 + 16]]
+        return found[:-1] if isinstance(step, int) and (step, part) == (7, 1) else found
 
 
 def exchange_kernel(
@@ -121,7 +122,7 @@
     barrier = pltpu.get_barrier_semaphore()
 
     def greet(step, part):
-        for where in partners.layer(step)[part * 16 : part * 16 + 16]:
+        for where in partners.half_plane(step, part):
             pl.semaphore_signal(barrier, inc=1, device_id=where, device_id_type=MESH)
 
     def load(k, frames):
@@ -135,11 +136,14 @@
 
     proto_copy = pltpu.make_async_copy(proto_hbm, proto_ref, proto_sem)
     proto_copy.start()
-    for step in range(GREETED):
+    for step in range(2):
         greet(step, 0)
+    load(0, range(FRAMES))
+    for step in range(2, 5):
+        greet(step, 0)
+    load(1, range(FRAMES))
+    for step in range(3):
         greet(step, 1)
-        if step < 2:
-            load(step, range(FRAMES))
     w_copy = pltpu.make_async_copy(w_hbm, w_buf, w_sem)
     proto_copy.wait()
 
@@ -180,10 +184,11 @@
         turns = TILES // 2
 
         def two_tiles(turn, carry):
-            step = GREETED + k * turns + turn
             for part in range(2):
-                if k == 0 or (k == 1 and turn == 0):
-                    greet(step, part)
+                if k == 0:
+                    greet(3 + turn if part else 5 + turn, part)
+                elif k == 1:
+                    greet(*((7, 0), (5, 1), (6, 1), (7, 1))[turn * 2 + part])
                 if k + 2 < CHUNKS:
                     share = FRAMES // TILES
                     load(k + 2, [(turn * 2 + part) * share + f for f in range(share)])
@@ -243,34 +248,35 @@
     def _():
         edge_copy.start()
 
-    def send(step, half):
-        for where in partners.layer(step):
-            pltpu.make_async_remote_copy(
-                src_ref=leaving.at[half, where[0] * BLOCKS + where[1]],
-                dst_ref=moved.at[half, me],
-                send_sem=send_sem,
-                recv_sem=recv_sem,
-                device_id=where,
-                device_id_type=MESH,
-            ).start()
-
-    def send_planes(half, first, last):
-        def plane(step, carry):
-            send(step, half)
-            return carry
-
-        if first < 7:
-            lax.fori_loop(first, min(last, 7), plane, 0)
-        if last == 8:
-            send(7, half)
-
-    far = 4
-    send_planes(1, 0, far)
+    def send(runs, half):
+        def half_plane(step, part):
+            for where in partners.half_plane(step, part):
+                pltpu.make_async_remote_copy(
+                    src_ref=leaving.at[half, where[0] * BLOCKS + where[1]],
+                    dst_ref=moved.at[half, me],
+                    send_sem=send_sem,
+                    recv_sem=recv_sem,
+                    device_id=where,
+                    device_id_type=MESH,
+                ).start()
+
+        for part, first, last in runs:
+            if last == 8:
+                half_plane(7, part)
+            else:
+
+                def body(step, carry):
+                    half_plane(step, part)
+                    return carry
+
+                lax.fori_loop(first, last, body, 0)
+
+    send(FAR, 1)
     transform(0, 2)
 
     @pl.when(block == 2)
     def _():
-        send_planes(1, far, 8)
+        send(NEAR, 1)
 
     @pl.when(block > 0)
     def _():
@@ -281,13 +287,13 @@
         rows_buf[pl.ds(parity * 2, PAIRS, stride=4), :] = value
     early = rows_buf[pl.ds(0, 2 * BAND), :].reshape(BAND, 2, LANES)
     leaving[0] = early.astype(jnp.bfloat16)
-    send_planes(0, 0, far)
+    send(FAR, 0)
 
     @pl.when(block != 2)
     def _():
-        send_planes(1, far, 8)
-
-    send_planes(0, far, 8)
+        send(NEAR, 1)
+
+    send(NEAR, 0)
     for half in range(2):
         pltpu.make_async_copy(leaving.at[half, me], moved.at[half, me], recv_sem).start()
 
@@ -357,19 +363,27 @@
 
     wide = lax.broadcasted_iota(jnp.int32, (LANES, LANES), 1)
     copies = []
-    for group in range(8):
-        columns = pl.ds(group * LANES, LANES)
-        square = gathered[:, columns].T
-        other = pltpu.roll(square, 64, 1)
-        other = jnp.where(wide < 64, other, -other)
-        for part, left in enumerate((square, other)):
-            product = jnp.dot(
-                left.astype(jnp.bfloat16), right[...], preferred_element_type=jnp.float32
-            )
-            out_buf[0, part, columns, :] = (product * (1.0 / 64.0)).astype(jnp.bfloat16)
+    size = 1 * LANES
+    for turn in range(8 // 1):
+        lefts = ([], [])
+        for group in range(turn * 1, turn * 1 + 1):
+            square = gathered[:, pl.ds(group * LANES, LANES)].T
+            other = pltpu.roll(square, 64, 1)
+            lefts[0].append(square.astype(jnp.bfloat16))
+            lefts[1].append(jnp.where(wide < 64, other, -other).astype(jnp.bfloat16))
+        product = jnp.dot(
+            jnp.concatenate(lefts[0] + lefts[1], axis=0),
+            right[...],
+            preferred_element_type=jnp.float32,
+        )
+        rows = pl.ds(turn * size, size)
+        for part in range(2):
+            out_buf[0, part, rows, :] = (
+                product[part * size : (part + 1) * size] * (1.0 / 64.0)
+            ).astype(jnp.bfloat16)
         copies.append(
             pltpu.make_async_copy(
-                out_buf.at[:, :, columns, :], out_hbm.at[:, :, columns, :], out_sem.at[group]
+                out_buf.at[:, :, rows, :], out_hbm.at[:, :, rows, :], out_sem.at[turn]
             )
         )
         copies[-1].start()

time: 28.4 us -> 27.8 us (0.979)
  Pallas kernels: 28.3 us -> 27.6 us
    pallas_call x1, Pallas kernels: 25.4 us -> 24.8 us  [exchange(): pl.pallas_call(exchange_kernel, out_shape=jax.ShapeDtypeStruct((2, DEVICE...]
where the time goes in v5:
time: 27.8 us; the launch traced here: 27.7 us
  Pallas kernels  27.6 us (99%)
    pallas_call x1, Pallas kernels, exchange(): pl.pallas_call(exchange_kernel, out_shape=jax.ShapeDtypeStruct((2, DEVICE...  24.8 us
    pallas_call x1, Pallas kernels, correlate(): pl.pallas_call(correlate_kernel, out_shape=jax.ShapeDtypeStruct(shape, jn...  2.83 us

profile of v5, /device:TPU:1, one launch (start us, length us, event | category | flops | bytes accessed | tf_op | source)
XLA Modules:
  0.0 27.7 jit_solution(9853887572553213605)
XLA Ops:
  0.0 24.8 %channelize_and_send.1.moved_ref = bf16[2,256,2,128]{3,2,1,0:T(2,128)(2,1)S(1)} custom-call(bf16[2,16,65536]{2,1,0:T(8,128)(2,1)} %v_hbm.1, f32[4,4096]{1,0:T(4,128)} %proto_hbm.1, bf16[2,256,2048]{2,1,0:T(8,128)(2,1)} %constant.2.clone.w_hbm), custom_call_target="tpu_custom_call" | custom-call | tf_op jit(solution)/shard_map/channelize_and_send/pallas_call | solution.py:311
  24.8 2.8 %correlate.1 = bf16[1,2,1024,1024]{3,2,1,0:T(8,128)(2,1)} custom-call(bf16[2,256,2,128]{3,2,1,0:T(2,128)(2,1)S(1)} %channelize_and_send.1.moved_ref), custom_call_target="tpu_custom_call" | custom-call | tf_op jit(solution)/shard_map/correlate/pallas_call | solution.py:397

commit v6 on v5

--- a/solution.py
+++ b/solution.py
@@ -200,7 +200,7 @@
                 two_tiles(turn, 0)
         else:
             lax.fori_loop(0, turns, two_tiles, 0)
-        if k == 1:
+        if k == 0:
             w_copy.start()
 
     w_copy.wait()
@@ -356,21 +356,19 @@
                 tile = pltpu.roll(tile, 0, 1, stride=INPUTS, stride_axis=0)
                 tile = jnp.take_along_axis(tile, source, axis=0)
                 tile = jnp.take_along_axis(tile, back, axis=1)
-                at = (block * 4 + quad) * QUAD
-                gathered[pl.ds(at, QUAD), columns] = tile[:QUAD]
-                gathered[pl.ds(64 + at, QUAD), columns] = tile[QUAD:]
+                gathered[pl.ds((block * 4 + quad) * 8, 8), columns] = tile
     right[...] = gathered[...].astype(jnp.bfloat16)
 
-    wide = lax.broadcasted_iota(jnp.int32, (LANES, LANES), 1)
+    imaginary = lax.rem(lax.broadcasted_iota(jnp.int32, (LANES, LANES), 1), 8) >= QUAD
     copies = []
     size = 1 * LANES
     for turn in range(8 // 1):
         lefts = ([], [])
         for group in range(turn * 1, turn * 1 + 1):
             square = gathered[:, pl.ds(group * LANES, LANES)].T
-            other = pltpu.roll(square, 64, 1)
+            forward, backward = pltpu.roll(square, LANES - QUAD, 1), pltpu.roll(square, QUAD, 1)
             lefts[0].append(square.astype(jnp.bfloat16))
-            lefts[1].append(jnp.where(wide < 64, other, -other).astype(jnp.bfloat16))
+            lefts[1].append(jnp.where(imaginary, -backward, forward).astype(jnp.bfloat16))
         product = jnp.dot(
             jnp.concatenate(lefts[0] + lefts[1], axis=0),
             right[...],

time: 27.8 us -> 27.9 us (level)
  no operation moved by 1% of the time
where the time goes in v6:
time: 27.9 us; the launch traced here: 27.7 us
  Pallas kernels  27.7 us (99%)
    pallas_call x1, Pallas kernels, exchange(): pl.pallas_call(exchange_kernel, out_shape=jax.ShapeDtypeStruct((2, DEVICE...  25 us
    pallas_call x1, Pallas kernels, correlate(): pl.pallas_call(correlate_kernel, out_shape=jax.ShapeDtypeStruct(shape, jn...  2.78 us

profile of v6, /device:TPU:1, one launch (start us, length us, event | category | flops | bytes accessed | tf_op | source)
XLA Modules:
  0.0 27.7 jit_solution(13556345705791990001)
XLA Ops:
  0.0 25.0 %channelize_and_send.1.moved_ref = bf16[2,256,2,128]{3,2,1,0:T(2,128)(2,1)S(1)} custom-call(bf16[2,16,65536]{2,1,0:T(8,128)(2,1)} %v_hbm.1, f32[4,4096]{1,0:T(4,128)} %proto_hbm.1, bf16[2,256,2048]{2,1,0:T(8,128)(2,1)} %constant.2.clone.w_hbm), custom_call_target="tpu_custom_call" | custom-call | tf_op jit(solution)/shard_map/channelize_and_send/pallas_call | solution.py:311
  25.0 2.8 %correlate.1 = bf16[1,2,1024,1024]{3,2,1,0:T(8,128)(2,1)} custom-call(bf16[2,256,2,128]{3,2,1,0:T(2,128)(2,1)S(1)} %channelize_and_send.1.moved_ref), custom_call_target="tpu_custom_call" | custom-call | tf_op jit(solution)/shard_map/correlate/pallas_call | solution.py:395
